TPU v7x, 32 devices: a whole 2x2x4 slice. The times are simulated.
32 devices in a mesh: dom: 8 (over y, x, core), harm: 4 (over z).
Axes of the slice: x: 2, y: 2, z: 4, core: 2. Of those that a mesh axis runs over, the one named last changes fastest.
Arguments:
- basis: float32 [20, 2, 256, 16384], P(None, None, 'harm', 'dom'), may hold values from -200 to 200, as said below
- coeffs: float32 [20], replicated, may hold values from -4 to 4
- conductance_tiles: float32 [128, 6, 128, 128], P('dom'), may hold values from -0.21875 to 0.21875
- tile_cols: int32 [128, 6], P('dom'), may hold values from 0 to 23, as said below
- self_cond: float32 [16384], P('dom'), may hold values from 1.5 to 4
- cap: float32 [16384], P('dom'), may hold values from 0.05 to 0.5
- send_nodes: int32 [8, 8, 128], P('dom'), may hold values from 0 to 2047, as said below
- send_count: int32 [8, 8], P('dom'), may hold values from 0 to 128, as said below
- nl_nodes: int32 [8, 512], P('dom'), may hold values from 0 to 2047, as said below
- nl_count: int32 [8], P('dom'), may hold values from 1 to 512, 2048 in all
- op_wave: float32 [512, 4096], P(None, ('dom', 'harm')), may hold values from -1.5 to 1
- nl_gain: float32 [4096], P(('dom', 'harm')), may hold values from 0.1 to 1
Outputs:
- new_vector: float32 [2, 256, 16384], P(None, 'harm', 'dom')
- hess_column: float32 [21], replicated
Inputs may be any that keep to these rules, and one draw needn't show every extreme that they name: `send_count`: A partition s lists live nodes only for the partitions 1, 7, 4 and 5 places after it (modulo 8), never for itself, at least 32 for each of those, and exactly 128 for at least one of them. `send_nodes`: distinct local nodes within one list. `tile_cols`: every tile of the ghost part of each partition's extended vector is read by some row tile of that partition. `nl_nodes`: distinct local nodes within a partition. The basis vectors are linearly independent.
All inputs are finite; a program needn't handle non-finite values. No bound on the sum of `nl_count` on one device may be relied on, other than what follows from the above.
Results may differ from a plain program's by a relative error of at most 0.0003.
Values sent between devices are 32-bit elements; how exact they have to be, the bound alone decides.
A program may use at most 128 MiB of HBM per device.

v0:
```python
import math

import jax
import jax.numpy as jnp
from jax import lax
from jax.sharding import PartitionSpec as P

HARM = 256


epsilon = 1e-06


def tables(harmonic, samples):
    sample_index = jnp.arange(samples, dtype=jnp.int32)
    product = harmonic[None, :] * sample_index[:, None] % samples
    angles = 2.0 * math.pi * product.astype(jnp.float32) / samples
    cosine = jnp.cos(angles)
    sine_part = jnp.sin(angles)
    alternating = 1.0 - 2.0 * (sample_index % 2).astype(jnp.float32)
    is_zero = harmonic == 0
    second = jnp.where(is_zero[None, :], alternating[:, None], sine_part)
    inverse = jnp.stack([cosine, second], axis=1)
    weights = jnp.where(is_zero, 1.0 / samples, 2.0 / samples).astype(jnp.float32)
    forward = jnp.transpose(
        jnp.stack([cosine * weights[None, :], second * weights[None, :]], axis=1), (1, 2, 0)
    )
    return (inverse, forward)


def solve_gram(gram_matrix, projections):
    factor = jnp.linalg.cholesky(gram_matrix)
    size_count = gram_matrix.shape[0]
    middle = jnp.zeros_like(projections)
    for index in range(size_count):
        middle = middle.at[index].set(
            (projections[index] - jnp.dot(factor[index], middle, precision=lax.Precision.HIGHEST))
            / factor[index, index]
        )
    answer = jnp.zeros_like(projections)
    for index in range(size_count - 1, -1, -1):
        answer = answer.at[index].set(
            (middle[index] - jnp.dot(factor[:, index], answer, precision=lax.Precision.HIGHEST))
            / factor[index, index]
        )
    return answer


def local(
    basis,
    coeffs,
    conductance_tiles,
    tile_cols,
    self_cond,
    cap,
    send_nodes,
    send_count,
    nl_nodes,
    nl_count,
    op_wave,
    nl_gain,
):
    highest_harmonic = lax.Precision.HIGHEST
    harm_local = basis.shape[2]
    node_dev = basis.shape[3]
    count_of_rows = 2 * harm_local
    peer_count = lax.axis_size("dom")
    vector = jnp.einsum("b,bpkn->pkn", coeffs, basis, precision=highest_harmonic)
    flattened = vector.reshape(count_of_rows, node_dev)
    peer_cap = send_nodes.shape[2]
    active = jnp.arange(peer_cap, dtype=jnp.int32)[None, :] < send_count[0][:, None]
    packed = jnp.take(flattened, send_nodes[0].reshape(-1), axis=1).reshape(
        count_of_rows, peer_count, peer_cap
    )
    packed = jnp.where(active[None], packed, 0.0)
    ghosts = lax.all_to_all(packed, "dom", split_axis=1, concat_axis=1, tiled=True)
    tile_size = conductance_tiles.shape[2]
    local_tiles = node_dev // tile_size
    extended = jnp.concatenate(
        [flattened.reshape(count_of_rows, local_tiles, tile_size), ghosts], axis=1
    )
    picked_entries = jnp.take(extended, tile_cols, axis=1)
    coupled_nodes = jnp.einsum(
        "rhfq,hfqo->rho", picked_entries, conductance_tiles, precision=highest_harmonic
    ).reshape(2, harm_local, node_dev)
    harmonic = lax.axis_index("harm") * harm_local + jnp.arange(harm_local, dtype=jnp.int32)
    angular = 2.0 * math.pi * harmonic.astype(jnp.float32) / HARM
    frequency = jnp.stack(
        [-angular[:, None] * cap[None, :] * vector[1], angular[:, None] * cap[None, :] * vector[0]]
    )
    base = coupled_nodes + self_cond[None, None, :] * vector + frequency
    nl_cap = nl_nodes.shape[1]
    nl_active = jnp.arange(nl_cap, dtype=jnp.int32) < nl_count[0]
    sampled = jnp.where(nl_active[None, None, :], jnp.take(vector, nl_nodes[0], axis=2), 0.0)
    samples = 2 * HARM
    node_conductance = nl_gain[None, :] * jnp.exp(op_wave)
    inverse, forward = tables(harmonic, samples)
    inverse_local = inverse.reshape(samples, count_of_rows)
    forward_local = forward.reshape(count_of_rows, samples)
    sampled_rows = sampled.reshape(count_of_rows, nl_cap)
    waveform_rows = lax.psum_scatter(
        jnp.einsum("cn,sc->ns", sampled_rows, inverse_local, precision=highest_harmonic),
        "harm",
        scatter_dimension=0,
        tiled=True,
    )
    current_rows = waveform_rows * node_conductance.T
    returned_rows = jnp.dot(
        lax.all_gather(current_rows, "harm", axis=0, tiled=True),
        forward_local.T,
        precision=highest_harmonic,
    )
    back_local = returned_rows.T.reshape(2, harm_local, nl_cap)
    back_local = jnp.where(nl_active[None, None, :], back_local, 0.0)
    product = base.at[:, :, nl_nodes[0]].add(back_local)
    gram_local = jnp.einsum("apkn,bpkn->ab", basis, basis, precision=highest_harmonic)
    proj_local = jnp.einsum("apkn,pkn->a", basis, product, precision=highest_harmonic)
    entries = count_of_rows * lax.axis_size("harm") * node_dev * peer_count
    gram_matrix, projections, energy = lax.psum(
        (gram_local, proj_local, jnp.sum(product * product)), ("dom", "harm")
    )
    hess = solve_gram(gram_matrix / entries, projections / entries)
    residual = product - jnp.einsum("a,apkn->pkn", hess, basis, precision=highest_harmonic)
    mean_square = (energy - jnp.dot(projections, hess, precision=highest_harmonic)) / entries
    norm_value = jnp.sqrt(mean_square + epsilon)
    return (residual / norm_value, jnp.concatenate([hess, norm_value[None]]))


def solution(mesh):
    in_specs = (
        P(None, None, "harm", "dom"),
        P(),
        P("dom", None, None, None),
        P("dom", None),
        P("dom"),
        P("dom"),
        P("dom", None, None),
        P("dom", None),
        P("dom", None),
        P("dom"),
        P(None, ("dom", "harm")),
        P(("dom", "harm")),
    )
    out_specs = (P(None, "harm", "dom"), P())
    return jax.shard_map(local, mesh=mesh, in_specs=in_specs, out_specs=out_specs, check_vma=False)
```

profile of v0, /device:TPU:0, one launch (start us, length us, event | category | flops | bytes accessed | tf_op | source)
XLA Modules:
  0.0 453.5 jit_solution(7828179183302353014)
XLA Ops:
  7.2 0.6 copy-done
  7.8 31.5 %fusion.2 = f32[1,2,64,2048]{3,0,2,1:T(1,128)S(1)} fusion(f32[20,2,64,2048]{3,2,1,0:T(8,128)} %param.92, f32[20]{0:T(128)S(1)} %copy-done), kind=kOutput, calls=%fused_computation.6 | convolution fusion | flops 62914560 | bytes 22020176 | tf_op jit(solution)/shard_map/b,bpkn->pkn/dot_general | solution.py:68
  39.3 2.5 copy.59
  41.9 2.3 copy.42
  44.2 1.5 copy.43
  45.8 4.0 gather_fusion
  49.8 1.2 copy.44
  51.2 0.9 select_select_fusion
  52.1 5.2 %all-to-all-start = ((f32[128,8,128]{2,0,1:T(8,128)}), f32[128,8,128]{2,0,1:T(8,128)}, u32[]{:S(2)}, u32[]{:S(2)}) async-start(f32[128,8,128]{2,0,1:T(8,128)} %select_select_fusion), calls=%async_computation | async-start | bytes 1048576 | tf_op jit(solution)/shard_map/all_to_all | solution.py:76
  57.2 11.6 %reduce-scatter.2.cloned.1.call-start = ((), (), s32[]{:S(2)}) async-start(), calls=%async_computation.2 | async-start | bytes 1310720 | tf_op jit(solution)/shard_map/reduce_scatter | solution.py:101
  69.5 2.1 gather_fusion.2
  72.3 2.4 select_bitcast_fusion
  74.7 1.3 broadcast_multiply_fusion
  76.0 2.1 convolution_bitcast_fusion
  78.1 1.1 reshape.1528
  79.3 1.3 copy.45
  81.3 1.1 copy.50
  82.4 6.7 %slice_multiply_fusion.1 = (f32[1,64,2048]{1,0,2:T(1,128)S(1)}, f32[1,64,2048]{1,0,2:T(1,128)}) fusion(f32[2,64,2048]{1,0,2:T(2,128)S(1)} %bitcast.296, f32[64]{0:T(128)S(1)} %fusion.90, f32[2048]{0:T(1024)S(1)} %copy-done.11, f32[64]{0:T(128)S(1)} %get-tuple-element.572), kind=kLoop, calls=%fused_computation.29 | loop fusion | flops 524288 | bytes 2105856 | tf_op jit(solution)/shard_map/mul | solution.py:89
  89.1 57.3 %fusion.18 = f32[20,20]{0,1:T(8,128)S(1)} fusion(f32[20,2,64,2048]{3,2,1,0:T(8,128)} %param.92), kind=kOutput, calls=%fused_computation.26 | convolution fusion | flops 1258291200 | bytes 20973120 | tf_op jit(solution)/shard_map/apkn,bpkn->ab/dot_general | solution.py:116
  146.4 1.7 bitcast_multiply_fusion
  148.3 1.5 pad_maximum_fusion
  149.9 3.6 gather_fusion.1
  153.5 9.7 %fusion.14 = f32[128,16,128]{2,0,1:T(8,128)S(1)} fusion(f32[16,6,128,128]{3,2,1,0:T(8,128)} %param.94, f32[16,6,128,128]{3,2,1,0:T(8,128)} %bitcast.298, pred[16,6]{1,0:T(8,128)(4,1)S(1)} %copy.40), kind=kOutput, calls=%fused_computation.22 | convolution fusion | flops 2417491968 | bytes 13631584 | tf_op jit(solution)/shard_map/rhfq,hfqo->rho/dot_general | solution.py:83
  163.2 1.3 copy.150
  164.5 4.0 reshape.1529
  168.5 8.3 %maximum_add_fusion = f32[2,64,2048]{1,0,2:T(2,128)} fusion(f32[1,64,2048]{1,0,2:T(1,128)} %get-tuple-element.511, f32[1,64,2048]{1,0,2:T(1,128)S(1)} %get-tuple-element.510, f32[2,64,2048]{1,0,2:T(2,128)} %reshape.1529, f32[2048]{0:T(1024)S(1)} %copy-done.12, f32[1,2,64,2048]{2,1,3,0:T(2,128)S(1)} %copy-done.2), kind=kLoop, calls=%fused_computation.17 | loop fusion | flops 1048576 | bytes 4202496 | tf_op jit(solution)/shard_map/add | solution.py:91
  176.8 1.3 all-gather.2.cloned.1.call-done
  178.0 2.4 fusion.17
  180.7 16.7 %scatter_fusion = f32[2,64,2048]{1,0,2:T(2,128)S(1)} fusion(f32[2,64,2048]{1,0,2:T(2,128)S(1)} %copy-done.3, s32[512]{0:T(512)S(1)} %bitcast.302, f32[512,2,64]{2,1,0:T(2,128)S(1)} %copy.51), kind=kCustom, calls=%fused_computation.3 | custom fusion | flops 65536 | bytes 788480 | tf_op jit(solution)/shard_map/scatter-add | solution.py:115
  197.4 2.4 copy.61
  199.7 36.4 %fusion.21 = f32[20]{0:T(128)S(1)} fusion(f32[2,64,2048,1]{2,3,0,1:T(1,128)S(1)} %copy.61, f32[20,2,64,2048]{3,2,1,0:T(8,128)} %param.92), kind=kOutput, calls=%fused_computation.27 | convolution fusion | flops 62914560 | bytes 22020176 | tf_op jit(solution)/shard_map/apkn,pkn->a/dot_general | solution.py:117
  236.2 2.8 multiply_reduce_fusion
  239.0 40.5 %all-reduce.2 = (f32[20]{0:T(128)S(1)}, f32[20,20]{0,1:T(8,128)S(1)}, f32[]{:T(128)}) all-reduce(f32[20]{0:T(128)S(1)} %fusion.21, f32[20,20]{0,1:T(8,128)S(1)} %fusion.18, f32[]{:T(128)} %multiply_reduce_fusion), channel_id=1, replica_groups=mesh['dom'=8,'harm'=4] {'dom','harm'}, use_global_device_ids=true, to_apply=%region_2.3 | all-reduce | flops 421 | bytes 3368 | tf_op jit(solution)/shard_map/psum | solution.py:119
  280.0 0.7 fusion.93
  280.9 1.8 cholesky.18
  282.7 0.6 compare_reduce_fusion
  283.4 0.6 select_select_fusion.1
  284.0 0.6 fusion.82
  285.2 0.7 fusion.91
  291.1 1.4 fusion.78
  294.5 1.4 fusion.76
  297.8 1.3 fusion.74
  300.9 1.3 fusion.72
  304.1 1.4 fusion.70
  307.4 1.3 fusion.68
  310.6 1.4 fusion.66
  314.0 1.3 fusion.64
  317.3 1.3 fusion.62
  320.6 1.4 fusion.60
  324.0 1.4 fusion.58
  327.3 1.3 fusion.56
  330.5 1.4 fusion.54
  333.9 1.3 fusion.52
  337.1 1.4 fusion.50
  340.4 1.3 fusion.48
  343.6 1.3 fusion.46
  346.8 1.3 fusion.84
  348.1 0.7 fusion.92
  352.8 0.7 multiply_reduce_fusion.20
  354.8 0.6 multiply_reduce_fusion.19
  400.9 31.5 %fusion = f32[1,2,64,2048]{3,0,2,1:T(1,128)S(1)} fusion(f32[20,2,64,2048]{3,2,1,0:T(8,128)} %param.92, f32[20]{0:T(128)S(1)} %constant_dynamic-update-slice_fusion.36), kind=kOutput, calls=%fused_computation.4 | convolution fusion | flops 62914560 | bytes 22020176 | tf_op jit(solution)/shard_map/a,apkn->pkn/dot_general | solution.py:123
  433.0 3.2 copy.145
  437.6 4.4 fusion.13
  442.0 3.9 copy.56
  (129 shorter events, 17.2 us)
Async XLA Ops:
  7.2 0.7 copy-start
  41.8 40.6 %copy-start.1 = (f32[1,2,64,2048]{2,1,3,0:T(2,128)}, f32[1,2,64,2048]{2,1,3,0:T(2,128)S(1)}, u32[]{:S(2)}) copy-start(f32[1,2,64,2048]{2,1,3,0:T(2,128)S(1)} %copy.59) | copy-start | bytes 3145732
  41.8 3.9 copy-start.10
  45.8 5.3 %copy-start.17 = (s32[1,8]{1,0:T(1,128)S(1)}, s32[1,8]{1,0:T(1,128)}, u32[]{:S(2)}) copy-start(s32[1,8]{1,0:T(1,128)} %param.99) | copy-start | bytes 100
  49.8 19.1 %copy-start.13 = (s32[1,512]{1,0:T(1,128)S(1)}, s32[1,512]{1,0:T(1,128)}, u32[]{:S(2)}) copy-start(s32[1,512]{1,0:T(1,128)} %param.100) | copy-start | bytes 6148
  52.1 96.3 %all-to-all-start = ((f32[128,8,128]{2,0,1:T(8,128)}), f32[128,8,128]{2,0,1:T(8,128)}, u32[]{:S(2)}, u32[]{:S(2)}) async-start(f32[128,8,128]{2,0,1:T(8,128)} %select_select_fusion), calls=%async_computation | async-start | bytes 1048576 | tf_op jit(solution)/shard_map/all_to_all | solution.py:76
  57.2 89.2 %reduce-scatter.2.cloned.1.call-start = ((), (), s32[]{:S(2)}) async-start(), calls=%async_computation.2 | async-start | bytes 1310720 | tf_op jit(solution)/shard_map/reduce_scatter | solution.py:101
  68.9 0.6 copy-start.6
  72.3 5.8 %copy-start.14 = (pred[512]{0:T(512)(128)(4,1)}, pred[512]{0:T(512)(128)(4,1)S(1)}, u32[]{:S(2)}) copy-start(pred[512]{0:T(512)(128)(4,1)S(1)} %get-tuple-element.576) | copy-start | bytes 1540
  72.3 5.8 %copy-start.8 = (s32[16,6]{0,1:T(8,128)S(1)}, s32[16,6]{0,1:T(8,128)}, u32[]{:S(2)}) copy-start(s32[16,6]{0,1:T(8,128)} %param.95) | copy-start | bytes 1156
  78.1 100.0 %all-gather.2.cloned.1.call-start = ((), (), s32[]{:S(2)}) async-start(), calls=%async_computation.3 | async-start | bytes 1310720 | tf_op jit(solution)/shard_map/all_gather | solution.py:109
  79.3 3.1 copy-start.11
  89.1 57.3 %copy-start.18 = (f32[128]{0:T(128)S(1)}, f32[128]{0:T(128)}, u32[]{:S(2)}) copy-start(f32[128]{0:T(128)} %param.103) | copy-start | bytes 1540
  89.1 59.1 %copy-start.9 = (s32[16,6]{0,1:T(8,128)S(1)}, s32[16,6]{0,1:T(8,128)}, u32[]{:S(2)}) copy-start(s32[16,6]{0,1:T(8,128)} %param.95) | copy-start | bytes 1156
  89.1 59.2 %copy-start.16 = (s32[96]{0:T(128)S(1)}, s32[96]{0:T(128)}, u32[]{:S(2)}) copy-start(s32[96]{0:T(128)} %reshape.1371) | copy-start | bytes 1156
  164.5 4.0 copy-start.2
  164.5 4.0 copy-start.12
  168.5 9.5 %copy-start.5 = (f32[512,1,64]{0,2,1:T(8,128)S(1)}, f32[512,1,64]{0,2,1:T(8,128)}, u32[]{:S(2)}) copy-start(f32[512,1,64]{0,2,1:T(8,128)} %get-tuple-element.533) | copy-start | bytes 393220
  168.5 9.5 %copy-start.15 = (pred[512]{0:T(512)(128)(4,1)S(1)}, pred[512]{0:T(512)(128)(4,1)}, u32[]{:S(2)}) copy-start(pred[512]{0:T(512)(128)(4,1)} %copy-done.14) | copy-start | bytes 1540
  176.8 3.9 copy-start.3
  176.8 3.9 copy-start.7
  284.0 7.1 %copy-start.4 = (f32[20,20]{1,0:T(8,128)}, f32[20,20]{1,0:T(8,128)S(1)}, u32[]{:S(2)}) copy-start(f32[20,20]{1,0:T(8,128)S(1)} %select_select_fusion.1) | copy-start | bytes 4804
Sparse Core Ops, SparseCore 0:
  78.2 28.8 reduce-scatter.1
  148.3 29.6 all-gather.1
where the time goes:
time: 457 us; the launch traced here: 453 us
  matrix products  171 us (37%)
  between operations  92.8 us (20%)
  other arithmetic  88.4 us (19%)
  local copies, waits for them, and re-layouts  42.7 us (9%)
  blocking collectives  40.5 us (9%)
  starting transfers between devices  16.8 us (4%)
    dot_general x1, matrix products, local(): jnp.einsum('apkn,bpkn->ab', basis, basis, precision=highest_harmonic)  57.3 us
    psum x1, blocking collectives, local(): lax.psum((gram_local, proj_local, jnp.sum(product * product)), ('dom', 'h...  40.5 us
    dot_general x1, matrix products, local(): jnp.einsum('apkn,pkn->a', basis, product, precision=highest_harmonic)  36.4 us
    dot_general x1, matrix products, local(): jnp.einsum('a,apkn->pkn', hess, basis, precision=highest_harmonic)  31.5 us
    dot_general x1, matrix products, local(): jnp.einsum('b,bpkn->pkn', coeffs, basis, precision=highest_harmonic)  31.5 us
    dot_general x20, other arithmetic, solve_gram(): jnp.dot(factor[index], middle, precision=lax.Precision.HIGHEST)  25.2 us
    scatter-add x1, other arithmetic, local(): product = base.at[:, :, nl_nodes[0]].add(back_local)  16.7 us
    dot_general x20, other arithmetic, solve_gram(): jnp.dot(factor[:, index], answer, precision=lax.Precision.HIGHEST)  12.1 us
  transfers between devices with their start and end apart: 3, of which 1 were waited for; matrix products, arithmetic and copies ran while one was open for 23% of the time, Pallas kernels for 0%

commit v1 on v0

v1 whole, which is shorter than its diff:
```python
import functools
import math

import jax
import jax.numpy as jnp
import ml_dtypes
import numpy as np
from jax import lax
from jax.experimental import pallas as pl
from jax.experimental.pallas import tpu as pltpu
from jax.sharding import PartitionSpec as P

epsilon = 1e-06
BF = jnp.bfloat16
F32 = jnp.float32
HI = lax.Precision.HIGHEST
NT = (((1,), (1,)), ((), ()))


def dft_tables(groups, harm_local):
    harm = groups * harm_local
    samples = 2 * harm
    n = np.arange(samples)[:, None]
    k = np.arange(harm)[None, :]
    angle = 2.0 * np.pi * ((n * k) % samples) / samples
    cosine, sine = np.cos(angle), np.sin(angle)
    sine[:, 0] = 1.0 - 2.0 * (np.arange(samples) % 2)
    inverse = np.stack(
        [cosine.reshape(samples, groups, harm_local), sine.reshape(samples, groups, harm_local)],
        axis=2,
    ).reshape(samples, samples)
    weight = np.full((harm,), 2.0 / samples)
    weight[0] = 1.0 / samples
    weight = np.broadcast_to(
        weight.reshape(groups, 1, harm_local), (groups, 2, harm_local)
    ).reshape(samples)
    forward = (inverse * weight[None, :]).T

    def split(x):
        x = x.astype(np.float32)
        high = x.astype(ml_dtypes.bfloat16)
        low = (x - high.astype(np.float32)).astype(ml_dtypes.bfloat16)
        return [high, low]

    return np.stack(split(inverse) + split(forward))


def split2(x):
    high = x.astype(BF)
    return high, (x - high.astype(F32)).astype(BF)


def kernel(
    dims,
    basis_hbm, cond_hbm, wave_hbm, table_hbm, coef, cols, scount, ncount,
    selfc, cap, snodes, nnodes, gain,
    out_hbm, hess_ref,
    bv, cv, wv, tv, vec, ext_h, ext_l, oh, sacc, xs, xr, rs, rr, gs, gr, prod, outv,
    gmat, g1, g2, p1, p2, g2s, p2s, hspl,
    in_sem, aux_sem, out_sem,
    xs_sem, xr_sem, rs_sem, rr_sem, gs_sem, gr_sem,
    g1s_sem, g1r_sem, g2s_sem, g2r_sem, p1s_sem, p1r_sem, p2s_sem, p2r_sem,
):
    B, R, ND, NL, H, D, T, TPR, TILE, CAP = dims
    HL, SL = R // 2, NL // H
    RT = R * H
    CH = 256
    NCH = ND // CH
    offs = (1, D - 1, D // 2, D // 2 + 1)
    md = lax.axis_index("dom")
    mh = lax.axis_index("harm")
    entries = float(R * H * ND * D)

    def bcopy(c):
        lanes = pl.ds(pl.multiple_of(c * CH, CH), CH)
        return pltpu.make_async_copy(
            basis_hbm.at[:, :, lanes], bv.at[:, :, lanes], in_sem.at[c]
        )

    for c in range(NCH):
        bcopy(c).start()
    wcopy = pltpu.make_async_copy(wave_hbm, wv, aux_sem.at[0])
    tcopy = pltpu.make_async_copy(table_hbm, tv, aux_sem.at[1])
    ccopy = pltpu.make_async_copy(cond_hbm, cv, aux_sem.at[2])
    tcopy.start()
    wcopy.start()
    ccopy.start()

    dpeers = [lax.rem(md + j, D) for j in range(1, D)]
    hpeers = [lax.rem(mh + j, H) for j in range(1, H)]
    barrier = pltpu.get_barrier_semaphore()
    for p in dpeers:
        pl.semaphore_signal(barrier, inc=1, device_id=(p, mh), device_id_type=pl.DeviceIdType.MESH)
    for p in hpeers:
        pl.semaphore_signal(barrier, inc=1, device_id=(md, p), device_id_type=pl.DeviceIdType.MESH)

    lane = lax.broadcasted_iota(jnp.int32, (1, NL), 1)
    heads = [jnp.where(lane < ncount[0], nnodes[...], -1)]
    lane = lax.broadcasted_iota(jnp.int32, (1, CAP), 1)
    for off in offs:
        p = lax.rem(md + off, D)
        heads.append(jnp.where(lane < scount[0, p], snodes[pl.ds(p, 1), :], -1))
    head = jnp.concatenate(heads, axis=1)
    W = NL + 4 * CAP

    def build(c, carry):
        rows = lax.broadcasted_iota(jnp.int32, (64, W), 0) + c * 64
        oh[pl.ds(pl.multiple_of(c * 64, 64), 64), :] = jnp.where(rows == head, 1.0, 0.0).astype(BF)
        return carry

    lax.fori_loop(0, ND // 64, build, 0)
    for s in range(D):
        ext_h[T + s] = jnp.zeros((R, TILE), BF)
        ext_l[T + s] = jnp.zeros((R, TILE), BF)
    sacc[...] = jnp.zeros_like(sacc)

    def chunk(c, carry):
        bcopy(c).wait()
        lanes = pl.ds(pl.multiple_of(c * CH, CH), CH)

        def rows_step(r, carry2):
            rows = pl.ds(pl.multiple_of(r * 32, 32), 32)
            acc = coef[0] * bv[0, rows, lanes]
            for b in range(1, B):
                acc = acc + coef[b] * bv[b, rows, lanes]
            high, low = split2(acc)
            for i in range(CH // TILE):
                cut = slice(i * TILE, (i + 1) * TILE)
                vec[c * (CH // TILE) + i, rows, :] = acc[:, cut]
                ext_h[c * (CH // TILE) + i, rows, :] = high[:, cut]
                ext_l[c * (CH // TILE) + i, rows, :] = low[:, cut]
            return carry2

        lax.fori_loop(0, R // 32, rows_step, 0)
        high = jnp.concatenate([ext_h[c * 2], ext_h[c * 2 + 1]], axis=1)
        low = jnp.concatenate([ext_l[c * 2], ext_l[c * 2 + 1]], axis=1)
        both = jnp.concatenate([high, low], axis=0)
        got = jnp.dot(both, oh[lanes, :], preferred_element_type=F32)
        sacc[...] += got[:R] + got[R:]
        return carry

    lax.fori_loop(0, NCH, chunk, 0)

    pl.semaphore_wait(barrier, D - 1 + H - 1)

    def hcopy(src, dst, ssem, rsem, peer, slot):
        return pltpu.make_async_remote_copy(
            src_ref=src, dst_ref=dst.at[slot], send_sem=ssem.at[peer], recv_sem=rsem.at[slot],
            device_id=(md, peer), device_id_type=pl.DeviceIdType.MESH,
        )

    def dcopy(src, dst, ssem, rsem, peer, slot):
        return pltpu.make_async_remote_copy(
            src_ref=src, dst_ref=dst.at[slot], send_sem=ssem.at[peer], recv_sem=rsem.at[slot],
            device_id=(peer, mh), device_id_type=pl.DeviceIdType.MESH,
        )

    for h in range(H):
        xs[h] = sacc[:, h * SL:(h + 1) * SL]
    for p in hpeers:
        hcopy(xs.at[p], xr, xs_sem, xr_sem, p, mh).start()
    xr[mh] = xs[mh]

    def gcopy(j, off):
        return pltpu.make_async_remote_copy(
            src_ref=gs.at[j], dst_ref=gr.at[j], send_sem=gs_sem.at[j], recv_sem=gr_sem.at[j],
            device_id=(lax.rem(md + off, D), mh), device_id_type=pl.DeviceIdType.MESH,
        )

    for j, off in enumerate(offs):
        gs[j] = sacc[:, NL + j * CAP:NL + (j + 1) * CAP]
        gcopy(j, off).start()

    BG = 8 * B
    gmat[...] = jnp.zeros_like(gmat)

    def gram_step(g, carry):
        x = bv[:, pl.ds(pl.multiple_of(g * 8, 8), 8), :].reshape(BG, ND)
        high, low = split2(x)
        both = jnp.concatenate([high, low], axis=0)
        gmat[...] += lax.dot_general(high, both, NT, preferred_element_type=F32)
        return carry

    lax.fori_loop(0, R // 8, gram_step, 0)
    row = lax.broadcasted_iota(jnp.int32, (BG, BG), 0)
    col = lax.broadcasted_iota(jnp.int32, (BG, BG), 1)
    same = row % 8 == col % 8
    hh = jnp.where(same, gmat[:, :BG], 0.0)
    hl = jnp.where(same, gmat[:, BG:], 0.0)
    r2 = lax.broadcasted_iota(jnp.int32, (128, BG), 0)
    c2 = lax.broadcasted_iota(jnp.int32, (128, BG), 1)
    pick = jnp.where(r2 == c2 // 8, 1.0, 0.0)
    top = pick[:32]
    mid = jnp.dot(top, hh + hl, precision=HI, preferred_element_type=F32)
    mid = mid + lax.dot_general(top, hl, NT, precision=HI, preferred_element_type=F32)
    g1[md] = lax.dot_general(mid, pick, NT, precision=HI, preferred_element_type=F32)
    for p in dpeers:
        dcopy(g1.at[md], g1, g1s_sem, g1r_sem, p, md).start()

    wcopy.wait()
    tcopy.wait()
    wv[...] = gain[...] * jnp.exp(wv[...])

    for p in hpeers:
        hcopy(xs.at[p], xr, xs_sem, xr_sem, p, p).wait_recv()

    def transform(high_table, low_table, x):
        high, low = split2(x)
        both = jnp.concatenate([high, low], axis=1)
        y = jnp.dot(high_table, both, preferred_element_type=F32)
        z = jnp.dot(low_table, high, preferred_element_type=F32)
        return y[:, :SL] + y[:, SL:] + z

    waves = transform(tv[0], tv[1], xr[...].reshape(RT, SL))
    back = transform(tv[2], tv[3], wv[...] * waves)
    rs[...] = back.reshape(H, R, SL)
    for p in hpeers:
        hcopy(rs.at[p], rr, rs_sem, rr_sem, p, mh).start()
    rr[mh] = rs[mh]

    for p in dpeers:
        dcopy(g1.at[md], g1, g1s_sem, g1r_sem, p, p).wait_recv()
    g2[mh] = jnp.sum(g1[...], axis=0)
    for p in hpeers:
        hcopy(g2.at[mh], g2, g2s_sem, g2r_sem, p, mh).start()

    ccopy.wait()
    for j, off in enumerate(offs):
        gcopy(j, off).wait_recv()
        high, low = split2(gr[j])
        src = lax.rem(md + (D - off), D)
        ext_h[T + src] = high
        ext_l[T + src] = low
    harmonic = lax.broadcasted_iota(jnp.int32, (HL, TILE), 0) + mh * HL
    omega = 2.0 * math.pi * harmonic.astype(F32) / float(HL * H)

    def tile_step(t, carry):
        nodes = pl.ds(pl.multiple_of(t * TILE, TILE), TILE)
        highs = [ext_h[cols[t, i]] for i in range(TPR)]
        lows = [ext_l[cols[t, i]] for i in range(TPR)]
        both = jnp.concatenate(
            [jnp.concatenate(highs, axis=1), jnp.concatenate(lows, axis=1)], axis=0
        )
        ch, cl = split2(cv[t].reshape(TPR * TILE, TILE))
        y = jnp.dot(both, jnp.concatenate([ch, cl], axis=1), preferred_element_type=F32)
        y = y[:R] + y[R:]
        y = y[:, :TILE] + y[:, TILE:]
        v = vec[t]
        y = y + selfc[:, nodes] * v
        turn = omega * cap[:, nodes]
        prod[0:HL, nodes] = y[:HL] - turn * v[HL:]
        prod[HL:R, nodes] = y[HL:] + turn * v[:HL]
        return carry

    lax.fori_loop(0, T, tile_step, 0)

    for p in hpeers:
        hcopy(g2.at[mh], g2, g2s_sem, g2r_sem, p, p).wait_recv()
    ri = lax.broadcasted_iota(jnp.int32, (32, 128), 0)
    ci = lax.broadcasted_iota(jnp.int32, (32, 128), 1)
    work = jnp.sum(g2[...], axis=0) / entries + jnp.where((ci == ri + 64) & (ri < B), 1.0, 0.0)
    diag = jnp.ones((32, 1), F32)
    for k in range(B):
        pivot = work[k:k + 1, k:k + 1]
        diag = jnp.where(ri[:, :1] == k, pivot, diag)
        factor = jnp.where(ri[:, :1] > k, work[:, k:k + 1] / pivot, 0.0)
        work = work - factor * work[k:k + 1, :]
    lower = jnp.concatenate([work[:, 64:], jnp.zeros((32, 64), F32)], axis=1)

    for p in hpeers:
        hcopy(rs.at[p], rr, rs_sem, rr_sem, p, p).wait_recv()
    rh, rl = split2(jnp.concatenate([rr[h] for h in range(H)], axis=1))
    both = jnp.concatenate([rh, rl], axis=0)

    def add_step(c, carry):
        lanes = pl.ds(pl.multiple_of(c * CH, CH), CH)
        y = lax.dot_general(both, oh[lanes, :NL], NT, preferred_element_type=F32)
        prod[:, lanes] += y[:R] + y[R:]
        return carry

    lax.fori_loop(0, NCH, add_step, 0)

    def fold(x):
        parts = [x[:, i * 128:(i + 1) * 128] for i in range(x.shape[1] // 128)]
        while len(parts) > 1:
            parts = [a + b for a, b in zip(parts[::2], parts[1::2])]
        return parts[0]

    def proj_step(g, carry):
        rows = pl.ds(pl.multiple_of(g * 8, 8), 8)
        p = prod[rows, :]
        new = [carry[b] + fold(bv[b, rows, :] * p) for b in range(B)]
        new.append(carry[B] + fold(p * p))
        return tuple(new)

    accs = lax.fori_loop(0, R // 8, proj_step, tuple(jnp.zeros((8, 128), F32) for _ in range(B + 1)))
    sums = [jnp.sum(a, axis=0, keepdims=True) for a in accs]
    stack = jnp.concatenate(sums + [jnp.zeros((128 - B - 1, 128), F32)], axis=0)
    p1[md] = lax.dot_general(jnp.ones((8, 128), F32), stack, NT, precision=HI, preferred_element_type=F32)
    for p in dpeers:
        dcopy(p1.at[md], p1, p1s_sem, p1r_sem, p, md).start()
    for p in dpeers:
        dcopy(p1.at[md], p1, p1s_sem, p1r_sem, p, p).wait_recv()
    p2[mh] = jnp.sum(p1[...], axis=0)
    for p in hpeers:
        hcopy(p2.at[mh], p2, p2s_sem, p2r_sem, p, mh).start()
    for p in hpeers:
        hcopy(p2.at[mh], p2, p2s_sem, p2r_sem, p, p).wait_recv()
    total = jnp.sum(p2[...], axis=0)[:1] / entries
    li = ci[:1]
    energy = jnp.sum(jnp.where(li == B, total, 0.0), axis=1, keepdims=True)
    proj = jnp.where(li < B, total, 0.0)
    y = jnp.sum(lower * proj, axis=1, keepdims=True)
    z = y / diag
    hess = jnp.sum(lower * z, axis=0, keepdims=True)
    square = energy - jnp.sum(proj * hess, axis=1, keepdims=True)
    norm = jnp.sqrt(square + epsilon)
    hess_ref[...] = jnp.where(li == B, norm, hess)
    for b in range(B):
        one = jnp.sum(jnp.where(li == b, hess, 0.0), axis=1, keepdims=True)
        hspl[b] = jnp.broadcast_to(one, (8, 128))
    hspl[B] = jnp.broadcast_to(1.0 / norm, (8, 128))

    WIDE = 1024
    scale = jnp.concatenate([hspl[B]] * (WIDE // 128), axis=1)

    def ocopy(q):
        rows = pl.ds(pl.multiple_of(q * 16, 16), 16)
        return pltpu.make_async_copy(outv.at[rows, :], out_hbm.at[rows, :], out_sem.at[q])

    def out_step(q, carry):
        for i in range(2):
            rows = pl.ds(pl.multiple_of(q * 16 + i * 8, 8), 8)
            for w in range(ND // WIDE):
                cut = slice(w * WIDE, (w + 1) * WIDE)
                acc = prod[rows, cut]
                for b in range(B):
                    acc = acc - jnp.concatenate([hspl[b]] * (WIDE // 128), axis=1) * bv[b, rows, cut]
                outv[rows, cut] = acc * scale
        ocopy(q).start()
        return carry

    lax.fori_loop(0, R // 16, out_step, 0)

    for p in hpeers:
        hcopy(xs.at[p], xr, xs_sem, xr_sem, p, mh).wait_send()
        hcopy(rs.at[p], rr, rs_sem, rr_sem, p, mh).wait_send()
        hcopy(g2.at[mh], g2, g2s_sem, g2r_sem, p, mh).wait_send()
        hcopy(p2.at[mh], p2, p2s_sem, p2r_sem, p, mh).wait_send()
    for p in dpeers:
        dcopy(g1.at[md], g1, g1s_sem, g1r_sem, p, md).wait_send()
        dcopy(p1.at[md], p1, p1s_sem, p1r_sem, p, md).wait_send()
    for j, off in enumerate(offs):
        gcopy(j, off).wait_send()
    for q in range(R // 16):
        ocopy(q).wait()


def local(
    basis, coeffs, conductance_tiles, tile_cols, self_cond, cap,
    send_nodes, send_count, nl_nodes, nl_count, op_wave, nl_gain,
):
    B, _, HL, ND = basis.shape
    R = 2 * HL
    T, TPR, TILE, _ = conductance_tiles.shape
    D, CAP = send_nodes.shape[1:]
    NL = nl_nodes.shape[1]
    H = lax.axis_size("harm")
    SL = NL // H
    S = R * H
    dims = (B, R, ND, NL, H, D, T, TPR, TILE, CAP)
    table = jnp.asarray(dft_tables(H, HL))
    any_ = pl.BlockSpec(memory_space=pl.ANY)
    vmem = pl.BlockSpec(memory_space=pltpu.VMEM)
    smem = pl.BlockSpec(memory_space=pltpu.SMEM)
    dma = pltpu.SemaphoreType.DMA
    V = pltpu.VMEM
    out, column = pl.pallas_call(
        functools.partial(kernel, dims),
        out_shape=(
            jax.ShapeDtypeStruct((R, ND), F32),
            jax.ShapeDtypeStruct((1, 128), F32),
        ),
        in_specs=[any_] * 4 + [smem] * 4 + [vmem] * 5,
        out_specs=(any_, vmem),
        scratch_shapes=[
            V((B, R, ND), F32),
            V(conductance_tiles.shape, F32),
            V((S, SL), F32),
            V((4, S, S), BF),
            V((T, R, TILE), F32),
            V((T + D, R, TILE), BF),
            V((T + D, R, TILE), BF),
            V((ND, NL + 4 * CAP), BF),
            V((R, NL + 4 * CAP), F32),
            V((H, R, SL), F32),
            V((H, R, SL), F32),
            V((H, R, SL), F32),
            V((H, R, SL), F32),
            V((4, R, CAP), F32),
            V((4, R, CAP), F32),
            V((R, ND), F32),
            V((R, ND), F32),
            V((8 * B, 16 * B), F32),
            V((D, 32, 128), F32),
            V((H, 32, 128), F32),
            V((D, 8, 128), F32),
            V((H, 8, 128), F32),
            V((8, 128), F32),
            V((8, 128), F32),
            V((B + 1, 8, 128), F32),
            dma((ND // 256,)), dma((3,)), dma((R // 16,)),
            dma((H,)), dma((H,)), dma((H,)), dma((H,)), dma((4,)), dma((4,)),
            dma((D,)), dma((D,)), dma((H,)), dma((H,)),
            dma((D,)), dma((D,)), dma((H,)), dma((H,)),
        ],
        compiler_params=pltpu.CompilerParams(
            collective_id=0, has_side_effects=True, vmem_limit_bytes=58 * 2**20
        ),
    )(
        basis.reshape(B, R, ND),
        conductance_tiles,
        op_wave,
        table,
        coeffs,
        tile_cols,
        send_count,
        nl_count,
        self_cond.reshape(1, ND),
        cap.reshape(1, ND),
        send_nodes.reshape(D, CAP),
        nl_nodes,
        nl_gain.reshape(1, SL),
    )
    return out.reshape(2, HL, ND), column[0, :B + 1]


def solution(mesh):
    in_specs = (
        P(None, None, "harm", "dom"),
        P(),
        P("dom", None, None, None),
        P("dom", None),
        P("dom"),
        P("dom"),
        P("dom", None, None),
        P("dom", None),
        P("dom", None),
        P("dom"),
        P(None, ("dom", "harm")),
        P(("dom", "harm")),
    )
    out_specs = (P(None, "harm", "dom"), P())
    return jax.shard_map(local, mesh=mesh, in_specs=in_specs, out_specs=out_specs, check_vma=False)
```

time: 457 us -> 56.6 us (0.12)
  matrix products: 171 us -> 0 us
  between operations: 92.8 us -> 1.29 us
  other arithmetic: 88.4 us -> 0 us
  Pallas kernels: 0 us -> 50.3 us
  blocking collectives: 40.5 us -> 0 us
  local copies, waits for them, and re-layouts: 42.7 us -> 4.77 us
  starting transfers between devices: 16.8 us -> 0 us
    dot_general x7 -> x0, matrix products: 171 us -> none  [the longest x1 57.3 us: local(): jnp.einsum('apkn,bpkn->ab', basis, basis, precision=highest_harmonic)]
    pallas_call x0 -> x1, Pallas kernels: none -> 50.3 us  [local(): pl.pallas_call(functools.partial(kernel, dims), out_shape=(jax.ShapeDtype...]
    psum x1 -> x0, blocking collectives: 40.5 us -> none  [local(): lax.psum((gram_local, proj_local, jnp.sum(product * product)), ('dom', 'h...]
    dot_general x41 -> x0, other arithmetic: 37.9 us -> none  [the longest x20 25.2 us: solve_gram(): jnp.dot(factor[index], middle, precision=lax.Precision.HIGHEST)]
    scatter-add x1 -> x0, other arithmetic: 16.7 us -> none  [local(): product = base.at[:, :, nl_nodes[0]].add(back_local)]
    reduce_scatter x1 -> x0, starting transfers between devices: 11.6 us -> none  [local(): lax.psum_scatter(jnp.einsum('cn,sc->ns', sampled_rows, inverse_local, pre...]
    gather x4 -> x0, local copies, waits for them, and re-layouts: 11 us -> none  [the longest x2 5.29 us: local(): jnp.take(flattened, send_nodes[0].reshape(-1), axis=1)]
    mul x3 -> x0, other arithmetic: 9.7 us -> none  [the longest x1 6.69 us: local(): -angular[:, None] * cap[None, :] * vector[1]]
  transfers between devices with their start and end apart: 3 -> 0, of which waited for: 1 -> 0; matrix products, arithmetic and copies ran while one was open for 23% -> 0% of each run, Pallas kernels for 0% -> 0%
where the time goes in v1:
time: 56.6 us; the launch traced here: 56.3 us
  Pallas kernels  50.3 us (89%)
  local copies, waits for them, and re-layouts  4.77 us (8%)
  between operations  1.29 us (2%)
    pallas_call x1, Pallas kernels, local(): pl.pallas_call(functools.partial(kernel, dims), out_shape=(jax.ShapeDtype...  50.3 us
    unnamed x2, local copies, waits for them, and re-layouts  3.66 us

profile of v1, /device:TPU:0, one launch (start us, length us, event | category | flops | bytes accessed | tf_op | source)
XLA Modules:
  0.0 56.3 jit_solution(16920213552503852902)
XLA Ops:
  1.3 1.4 %copy.15.cols = s32[16,6]{1,0:T(8,128)} copy(s32[16,6]{0,1:T(8,128)} %param.16) | data formatting | bytes 768 | tf_op args[3]
  2.6 50.3 %shard_map.140 = (f32[128,2048]{1,0:T(8,128)}, f32[1,128]{1,0:T(1,128)}) custom-call(f32[20,128,2048]{2,1,0:T(8,128)} %bitcast.8, f32[16,6,128,128]{3,2,1,0:T(8,128)} %cond_hbm.1, f32[512,128]{1,0:T(8,128)} %wave_hbm.1, bf16[4,512,512]{2,1,0:T(8,128)(2,1)} %constant.2.clone.table_hbm, f32[20]{0:T(128)} %coef.1, s32[16,6]{1,0:T(8,128)} %copy.15.cols, ...), custom_call_target="tpu_custom_call" | custom-call | tf_op jit(solution)/shard_map/pallas_call | solution.py:378
  52.9 1.1 %slice_bitcast_fusion = f32[21]{0:T(128)} fusion(f32[1,128]{1,0:T(1,128)} %get-tuple-element.5), kind=kLoop, calls=%fused_computation | loop fusion | bytes 168 | tf_op jit(solution)/shard_map/squeeze | solution.py:435
  54.0 2.3 %copy.18 = f32[2,64,2048]{2,1,0:T(8,128)} copy(f32[2,64,2048]{2,1,0:T(8,128)} %bitcast.9) | data formatting | bytes 2097152
